TPU v7x, 512 devices: a whole 4x8x8 slice. The times are simulated.
512 devices in a mesh: bin: 64 (over z, y), off: 8 (over x, core).
Axes of the slice: x: 4, y: 8, z: 8, core: 2. Of those that a mesh axis runs over, the one named last changes fastest.
Arguments:
- traces: float32 [8, 8192, 1536], P('off', 'bin'), may hold values from -6 to 6
- trace_dest: int32 [8, 8192, 1], P('off', 'bin'), may hold values from 0 to 63; in each aligned block of 128 rows (0 to 127, 128 to 255, ..., all dimensions but the last counted through in order) at most 6 rows name the same one
- trace_bin: int32 [8, 8192], P('off', 'bin'), may hold values from 0 to 31
- trace_class: int32 [8, 8192], P('off', 'bin'), may hold values from 0 to 7
- trace_fold: int32 [8, 8192], P('off', 'bin'), may hold values from 1 to 4
- filters: float32 [8, 48], replicated, may hold values from -0.3 to 0.3
- predictor: float32 [16, 1024], P(None, 'off'), may hold values from -0.4 to 0.4
Outputs:
- error_spectrum: float32 [2048, 1024], P('bin', 'off')
Inputs may be any that keep to these rules, and one draw needn't show every extreme that they name: `trace_dest`: in the 128 traces of one device (aligned blocks of rows, groups taken in order) no value is named by more than 6 traces, a bound that some block reaches.
All inputs are finite; a program needn't handle non-finite values.
Results may differ from a plain program's by a relative error of at most 0.0001.
Values sent between devices are 32-bit elements; how exact they have to be, the bound alone decides.
A program may use at most 128 MiB of HBM per device.

v0:
```python
import math

import jax
import jax.numpy as jnp
from jax import lax
from jax.sharding import PartitionSpec as P

BIN_DEV = 32


def passed_along(block, axis, distance):
    devices = range(lax.axis_size(axis))
    route = [(i - distance, i) for i in devices if i - distance in devices]
    return lax.ppermute(block, axis, route)


def deconvolve(records, per_trace):
    tap_count = per_trace.shape[1]
    samples = records.shape[1]
    padded = jnp.pad(records, ((0, 0), (tap_count, 0)))
    result = records
    for shift_by in range(1, tap_count + 1):
        result = (
            result
            - per_trace[:, shift_by - 1 : shift_by]
            * padded[:, tap_count - shift_by : tap_count - shift_by + samples]
        )
    return result


def pick_filters(class_ids, filters):
    one_hot = (class_ids[:, None] == jnp.arange(filters.shape[0], dtype=jnp.int32)[None, :]).astype(
        jnp.float32
    )
    return jnp.dot(
        one_hot, filters, precision=lax.Precision.HIGHEST, preferred_element_type=jnp.float32
    )


def dft_table(samples, first, count):
    times = jnp.arange(samples, dtype=jnp.int32)[:, None]
    freq_ids = first + jnp.arange(count, dtype=jnp.int32)[None, :]
    phase = freq_ids * times % samples
    angle = 2.0 * math.pi / samples * phase.astype(jnp.float32)
    factor = 1.0 / math.sqrt(samples)
    paired = jnp.stack([jnp.cos(angle) * factor, -jnp.sin(angle) * factor], axis=-1)
    return paired.reshape(samples, 2 * count)


def slot_layout(targets, bin_slots, class_ids, fold_counts, bin_devices, capacity):
    one_hot = (targets[:, None] == jnp.arange(bin_devices, dtype=jnp.int32)[None, :]).astype(
        jnp.int32
    )
    before = jnp.cumsum(one_hot, axis=0) - one_hot
    slot_rank = jnp.sum(before * one_hot, axis=1)
    slot_index = targets * capacity + slot_rank
    labels = jnp.stack([bin_slots, class_ids, fold_counts], axis=1)
    label_box = jnp.full((bin_devices * capacity, 3), -1, jnp.int32).at[slot_index].set(labels)
    return (slot_index, label_box.reshape(bin_devices, capacity, 3))


def stack_rows(got_rows, got_labels, width):
    flattened = got_rows.reshape(-1, width)
    flat_labels = got_labels.reshape(-1, 3)
    placing = (jnp.arange(BIN_DEV, dtype=jnp.int32)[:, None] == flat_labels[None, :, 0]).astype(
        jnp.float32
    )
    placing = placing * flat_labels[None, :, 2].astype(jnp.float32)
    stacked = jnp.dot(
        placing, flattened, precision=lax.Precision.HIGHEST, preferred_element_type=jnp.float32
    )
    return (stacked, jnp.sum(placing, axis=1))


def on_device(traces, trace_dest, trace_bin, trace_class, trace_fold, filters, predictor):
    records = traces[0]
    targets = trace_dest[0, :, 0]
    bin_slots = trace_bin[0]
    class_ids = trace_class[0]
    fold_counts = trace_fold[0]
    bin_devices = lax.axis_size("bin")
    samples = records.shape[1]
    lag_count = predictor.shape[0]
    local_freqs = predictor.shape[1] // 2
    capacity = max(2, 3 * records.shape[0] // bin_devices)
    slot_index, label_box = slot_layout(
        targets, bin_slots, class_ids, fold_counts, bin_devices, capacity
    )
    outbox = jnp.zeros((bin_devices * capacity, samples), jnp.float32).at[slot_index].set(records)
    part_records = lax.all_to_all(
        outbox.reshape(bin_devices, capacity, samples),
        "bin",
        split_axis=0,
        concat_axis=0,
        tiled=True,
    )
    part_labels = lax.all_to_all(label_box, "bin", split_axis=0, concat_axis=0, tiled=True)
    flattened = part_records.reshape(-1, samples)
    flat_labels = part_labels.reshape(-1, 3)
    cleaned_part = deconvolve(flattened, pick_filters(flat_labels[:, 1], filters))
    got_records = cleaned_part.reshape(part_records.shape)
    stacked, fold_total = stack_rows(got_records, part_labels, samples)
    stacked, fold_total = lax.psum((stacked, fold_total), "off")
    normal = stacked / jnp.sqrt(1.0 + fold_total)[:, None]
    own_table = dft_table(samples, lax.axis_index("off") * local_freqs, local_freqs)
    spectrum = jnp.dot(
        normal, own_table, precision=lax.Precision.HIGHEST, preferred_element_type=jnp.float32
    )
    lower_rim = passed_along(spectrum[-lag_count:], "bin", 1)
    extended = jnp.concatenate([lower_rim, spectrum], axis=0).reshape(-1, local_freqs, 2)
    coeffs = predictor.reshape(lag_count, local_freqs, 2)
    bin_total = spectrum.shape[0]
    guess_real = jnp.zeros((bin_total, local_freqs), jnp.float32)
    guess_imag = jnp.zeros((bin_total, local_freqs), jnp.float32)
    for lag_index in range(1, lag_count + 1):
        lagged = extended[lag_count - lag_index : lag_count - lag_index + bin_total]
        coeff_real = coeffs[lag_index - 1, :, 0]
        coeff_imag = coeffs[lag_index - 1, :, 1]
        guess_real = guess_real + coeff_real * lagged[:, :, 0] - coeff_imag * lagged[:, :, 1]
        guess_imag = guess_imag + coeff_real * lagged[:, :, 1] + coeff_imag * lagged[:, :, 0]
    current = spectrum.reshape(bin_total, local_freqs, 2)
    error_spectrum = jnp.stack(
        [current[:, :, 0] - guess_real, current[:, :, 1] - guess_imag], axis=-1
    )
    return error_spectrum.reshape(bin_total, 2 * local_freqs)


def solution(mesh):
    in_specs = (
        P("off", "bin", None),
        P("off", "bin", None),
        P("off", "bin"),
        P("off", "bin"),
        P("off", "bin"),
        P(),
        P(None, "off"),
    )
    out_specs = P("bin", "off")
    return jax.shard_map(
        on_device, mesh=mesh, in_specs=in_specs, out_specs=out_specs, check_vma=False
    )
```

profile of v0, /device:TPU:1, one launch (start us, length us, event | category | flops | bytes accessed | tf_op | source)
XLA Modules:
  0.0 259.3 jit_solution(8484560849659793734)
XLA Ops:
  6.5 0.8 fusion.209
  7.5 0.8 select_reduce_fusion
  8.4 0.7 fusion.230
  9.0 0.7 pad_add_fusion
  9.8 0.9 scatter_custom_fusion
  11.0 0.7 copy.130
  11.7 17.1 %all-to-all-start = ((s32[64,6,3]{1,2,0:T(4,128)}), s32[64,6,3]{1,2,0:T(4,128)S(1)}, u32[]{:S(2)}, u32[]{:S(2)}) async-start(s32[64,6,3]{1,2,0:T(4,128)} %copy.130), calls=%async_computation | async-start | bytes 262144 | tf_op jit(solution)/shard_map/all_to_all | solution.py:97
  28.9 1.7 scatter_custom_fusion.1
  30.6 1.8 reshape.659
  32.5 8.0 %all-to-all-done = s32[64,6,3]{1,2,0:T(4,128)S(1)} async-done(((s32[64,6,3]{1,2,0:T(4,128)}), s32[64,6,3]{1,2,0:T(4,128)S(1)}, u32[]{:S(2)}, u32[]{:S(2)}) %all-to-all-start) | async-done | bytes 4640 | tf_op jit(solution)/shard_map/all_to_all | solution.py:97
  40.4 5.6 %all-to-all-start.1 = ((f32[64,6,1536]{2,1,0:T(8,128)}), f32[64,6,1536]{2,1,0:T(8,128)}, u32[]{:S(2)}, u32[]{:S(2)}) async-start(f32[64,6,1536]{2,1,0:T(8,128)} %reshape.659), calls=%async_computation.1 | async-start | bytes 6291456 | tf_op jit(solution)/shard_map/all_to_all | solution.py:90
  46.3 1.7 cosine_multiply_fusion
  48.6 1.4 reshape.661
  50.2 3.2 %slice_reduce_fusion.30 = (f32[64]{0:T(128)S(1)}, f32[64]{0:T(128)S(1)}, f32[64]{0:T(128)S(1)}, f32[64]{0:T(128)S(1)}, f32[64]{0:T(128)S(1)}, /*index=5*/f32[64]...) fusion(f32[16,64,2]{0,2,1:T(2,128)S(1)} %bitcast.43), kind=kLoop, calls=%fused_computation.283 | loop fusion | bytes 6656 | tf_op jit(solution)/shard_map/slice | solution.py:118
  53.4 4.7 %slice_reduce_fusion.31 = (f32[64]{0:T(128)S(1)}, f32[64]{0:T(128)S(1)}, f32[64]{0:T(128)S(1)}, f32[64]{0:T(128)S(1)}, f32[64]{0:T(128)S(1)}, /*index=5*/f32[64]...) fusion(f32[16,64,2]{0,2,1:T(2,128)S(1)} %bitcast.44), kind=kLoop, calls=%fused_computation.284 | loop fusion | bytes 9728 | tf_op jit(solution)/shard_map/slice | solution.py:117
  58.8 14.5 %psum.15 = f32[32]{0:T(128)S(1)} all-reduce(f32[32]{0:T(128)S(1)} %select_reduce_fusion.1), channel_id=1, replica_groups=mesh['bin'=64,'off'=8] {'off'}, use_global_device_ids=true, to_apply=%region_6.7 | all-reduce | flops 32 | bytes 256 | tf_op jit(solution)/shard_map/psum | solution.py:103
  73.5 48.3 %all-to-all-done.1 = f32[64,6,1536]{2,1,0:T(8,128)} async-done(((f32[64,6,1536]{2,1,0:T(8,128)}), f32[64,6,1536]{2,1,0:T(8,128)}, u32[]{:S(2)}, u32[]{:S(2)}) %all-to-all-start.1) | async-done | bytes 2359328 | tf_op jit(solution)/shard_map/all_to_all | solution.py:90
  121.8 2.6 %reshape.660 = f32[384,1536]{1,0:T(8,128)S(1)} reshape(f32[64,6,1536]{2,1,0:T(8,128)} %all-to-all-done.1) | data formatting | bytes 4718592 | tf_op jit(solution)/shard_map/reshape | solution.py:98
  124.4 33.2 %fusion.257 = f32[384,1536]{1,0:T(8,128)S(1)} fusion(f32[384,1536]{1,0:T(8,128)S(1)} %reshape.660, f32[384]{0:T(512)S(1)} %get-tuple-element.6, f32[384]{0:T(512)S(1)} %get-tuple-element.7, f32[384]{0:T(512)S(1)} %get-tuple-element.8, f32[384]{0:T(512)S(1)} %get-tuple-element.9, f32[384]{0:T(512)S(1)} %get-tuple-element.10, ...), kind=kLoop, calls=%fused_computation.3.clone.2 | loop fusion | flops 56623104 | bytes 4792320 | tf_op jit(solution)/shard_map/dot_general | solution.py:69
  157.7 2.1 fusion
  159.8 81.6 %all-reduce.3.cloned.1.call-done = f32[32,1536]{1,0:T(8,128)} async-done(((f32[32,1536]{1,0:T(8,128)}), f32[32,1536]{1,0:T(8,128)}) %all-reduce.3.cloned.1.call-update) | async-done | bytes 196624 | tf_op jit(solution)/shard_map/psum | solution.py:103
  241.4 1.8 fusion.202
  243.4 2.4 collective-permute-start
  251.8 0.7 copy.186
  (103 shorter events, 8.3 us)
Async XLA Ops:
  6.5 22.4 %copy-start = (f32[1,128,1536]{2,1,0:T(8,128)S(1)}, f32[1,128,1536]{2,1,0:T(8,128)}, u32[]{:S(2)}) copy-start(f32[1,128,1536]{2,1,0:T(8,128)} %param.7) | copy-start | bytes 2359300
  11.7 28.7 %all-to-all-start = ((s32[64,6,3]{1,2,0:T(4,128)}), s32[64,6,3]{1,2,0:T(4,128)S(1)}, u32[]{:S(2)}, u32[]{:S(2)}) async-start(s32[64,6,3]{1,2,0:T(4,128)} %copy.130), calls=%async_computation | async-start | bytes 262144 | tf_op jit(solution)/shard_map/all_to_all | solution.py:97
  40.4 81.4 %all-to-all-start.1 = ((f32[64,6,1536]{2,1,0:T(8,128)}), f32[64,6,1536]{2,1,0:T(8,128)}, u32[]{:S(2)}, u32[]{:S(2)}) async-start(f32[64,6,1536]{2,1,0:T(8,128)} %reshape.659), calls=%async_computation.1 | async-start | bytes 6291456 | tf_op jit(solution)/shard_map/all_to_all | solution.py:90
  46.0 195.4 %all-reduce.3.cloned.1.call-start = ((), (), s32[]{:S(2)}) async-start(), calls=%async_computation.2 | async-start | bytes 393216 | tf_op jit(solution)/shard_map/psum | solution.py:103
  47.9 2.1 copy-start.2
  48.0 10.2 %copy-start.3 = (f32[8,48]{1,0:T(8,128)S(1)}, f32[8,48]{1,0:T(8,128)}, u32[]{:S(2)}) copy-start(f32[8,48]{1,0:T(8,128)} %param.12) | copy-start | bytes 4612
  157.6 83.8 %copy-start.1 = (f32[1536,128]{0,1:T(8,128)S(1)}, f32[1536,128]{0,1:T(8,128)}, u32[]{:S(2)}) copy-start(f32[1536,128]{0,1:T(8,128)} %reshape.661) | copy-start | bytes 2359300
  243.4 3.2 %collective-permute-start = (f32[16,128]{1,0:T(8,128)S(1)}, f32[16,128]{1,0:T(8,128)S(1)}, u32[]{:S(2)}, u32[]{:S(2)}) collective-permute-start(f32[16,128]{1,0:T(8,128)S(1)} %slice.877), channel_id=1, source_target_pairs={{0,8},{8,16},{16,24},{24,32},{32,40},{40,48},{48,56},{56,64},{64,7... | collective-permute-start | bytes 24584 | tf_op jit(solution)/shard_map/ppermute | solution.py:14
Sparse Core Ops, SparseCore 0:
  159.9 81.4 all-reduce.2
where the time goes:
time: 264 us; the launch traced here: 259 us
  waiting for transfers between devices  138 us (52%)
  other arithmetic  38.5 us (15%)
  starting transfers between devices  25.4 us (10%)
  local copies, waits for them, and re-layouts  24.3 us (9%)
  blocking collectives  14.5 us (5%)
  between operations  13.9 us (5%)
  matrix products  4.26 us (2%)
    psum x1, waiting for transfers between devices, on_device(): stacked, fold_total = lax.psum((stacked, fold_total), 'off')  81.6 us
    all_to_all x1, waiting for transfers between devices, on_device(): lax.all_to_all(outbox.reshape(bin_devices, capacity, samples), 'bin', spl...  48.3 us
    dot_general x1, other arithmetic, stack_rows(): jnp.dot(placing, flattened, precision=lax.Precision.HIGHEST, preferred_el...  33.2 us
    all_to_all x1, starting transfers between devices, on_device(): lax.all_to_all(label_box, 'bin', split_axis=0, concat_axis=0, tiled=True)  17.1 us
    psum x1, blocking collectives, on_device(): stacked, fold_total = lax.psum((stacked, fold_total), 'off')  14.5 us
    all_to_all x1, waiting for transfers between devices, on_device(): lax.all_to_all(label_box, 'bin', split_axis=0, concat_axis=0, tiled=True)  7.96 us
    all_to_all x1, starting transfers between devices, on_device(): lax.all_to_all(outbox.reshape(bin_devices, capacity, samples), 'bin', spl...  5.58 us
  transfers between devices with their start and end apart: 4, of which 4 were waited for; matrix products, arithmetic and copies ran while one was open for 6% of the time, Pallas kernels for 0%

commit v1 on v0

v1 whole, which is shorter than its diff:
```python
import math

import jax
import jax.numpy as jnp
import ml_dtypes
import numpy as np
from jax import lax
from jax.experimental import pallas as pl
from jax.experimental.pallas import tpu as pltpu
from jax.sharding import PartitionSpec as P

SAMPLES = 1536
HALF = SAMPLES // 2
TAPS = 48
LAGS = 16
BIN_DEV = 32
TR = 128
NZ, NY, NO = 8, 8, 8
GB = NY * BIN_DEV
WIDE = GB + 128
ROWS = 16
MESH = pl.DeviceIdType.MESH
F32, BF16 = jnp.float32, jnp.bfloat16


def split(v):
    high = v.astype(BF16)
    return high, (v - high.astype(F32)).astype(BF16)


def np_split(v):
    high = v.astype(np.float32).astype(ml_dtypes.bfloat16)
    low = (v - high.astype(np.float64)).astype(np.float32).astype(ml_dtypes.bfloat16)
    return high, low


def local_freqs():
    s, m = np.arange(NY)[:, None], np.arange(8)[None, :]
    return 2 * (8 * (s % (NY // 2)) + m) + (s >= NY // 2)


def tables():
    freqs = np.arange(NO)[:, None, None] * (NY * 8) + local_freqs()[None]

    def waves(count):
        phase = freqs[..., None] * np.arange(count) % SAMPLES
        angle = 2.0 * np.pi / SAMPLES * phase
        return np.stack([np.cos(angle), -np.sin(angle)], axis=2)

    main = waves(HALF) / math.sqrt(SAMPLES)
    main = main.reshape(NO, 2, NY // 2 * ROWS, HALF)
    main = np.concatenate(np_split(main), axis=2)
    high, low = np_split(waves(64).reshape(NO, NY * ROWS, 64))
    short = np.concatenate([high, low, high, np.zeros_like(high)], axis=2)
    place = np.zeros((NY * ROWS, NY * ROWS), np.float32)
    cols = 2 * local_freqs()[:, None, :] + np.arange(2)[None, :, None]
    place[np.arange(NY * ROWS), cols.reshape(-1)] = 1
    return main, short, place.astype(ml_dtypes.bfloat16)


def dot(a, b, da, db):
    return lax.dot_general(a, b, (((da,), (db,)), ((), ())), preferred_element_type=F32)


def kernel(
    traces, dest, slot, cls, fold, filt, pred, tab, gtab, place, out,
    xv, tv, gv, x2, pt, rv, rhs, lab0, lab1, lab2, sbuf, rbuf, lhs, hot, acc,
    obuf, obox, fbuf, fbox, ebuf, ebox, cv, cb, res,
    xsem, tsem, gsem, l1s, l1r, l2s, l2r, asend, arecv, bsend, brecv, fsend, frecv, esend, erecv,
):
    b, o = lax.axis_index("bin"), lax.axis_index("off")
    z, y = lax.div(b, NY), lax.rem(b, NY)

    def at(zz, yy, oo):
        return {"bin": zz * NY + yy, "off": oo}

    def remote(src, dst, ss, rs, where):
        return pltpu.make_async_remote_copy(
            src_ref=src, dst_ref=dst, send_sem=ss, recv_sem=rs, device_id=where, device_id_type=MESH
        )

    def await_bytes(ref, sem):
        pltpu.make_async_copy(ref, ref, sem).wait()

    pltpu.make_async_copy(traces.at[0], xv, xsem).start()

    def load(do, c):
        oo = lax.rem(o + do, NO)
        pltpu.make_async_copy(tab.at[oo], tv.at[do], tsem.at[do]).start()
        pltpu.make_async_copy(gtab.at[oo], gv.at[do], gsem.at[do]).start()
        return c

    lax.fori_loop(0, NO, load, 0)

    barrier = pltpu.get_barrier_semaphore()

    def greet(i, c):
        where = at(z, lax.rem(y + lax.rem(i, NY), NY), lax.rem(o + lax.div(i, NY), NO))
        pl.semaphore_signal(barrier, inc=1, device_id=where, device_id_type=MESH)
        return c

    def greet_z(dz, c):
        pl.semaphore_signal(
            barrier, inc=1, device_id=at(lax.rem(z + dz, NZ), y, o), device_id_type=MESH
        )
        return c

    lax.fori_loop(1, NO * NY, greet, 0)
    lax.fori_loop(1, NZ, greet_z, 0)
    lab0[0:1, :] = dest[...] * BIN_DEV + slot[...]
    lab0[1:2, :] = fold[...]
    pl.semaphore_wait(barrier, NO * NY - 1 + NZ - 1)

    pltpu.make_async_copy(lab0, lab1.at[o], l1r).start()

    def tell_off(do, c):
        remote(lab0, lab1.at[o], l1s, l1r, at(z, y, lax.rem(o + do, NO))).start()
        return c

    lax.fori_loop(1, NO, tell_off, 0)

    pltpu.make_async_copy(traces.at[0], xv, xsem).wait()
    first, second = xv[:, :HALF], xv[:, HALF:]
    for parity, v in ((0, first + second), (1, first - second)):
        high, low = split(v)
        x2[parity, 0:TR] = high
        x2[parity, TR : 2 * TR] = low
    pt[0:TAPS] = xv[:, SAMPLES - 128 :].T[128 - TAPS :]
    pt[TAPS:] = jnp.zeros((TAPS, TR), F32)
    class_hot = (lax.broadcasted_iota(jnp.int32, (8, TR), 0) == cls[...]).astype(F32)
    taps = lax.dot_general(
        filt[...].T, class_hot, (((1,), (0,)), ((), ())),
        precision=lax.Precision.HIGHEST, preferred_element_type=F32,
    )
    rv[...] = jnp.zeros_like(rv)
    rv[1 : TAPS + 1, 0:TR] = taps
    wrap = jnp.zeros((TAPS, TR), F32)
    for k in range(1, TAPS + 1):
        wrap = wrap + rv[k : k + 1, 0:TR] * pt[TAPS - k : 2 * TAPS - k]
    rv[0:TAPS, TR:] = wrap * (1.0 / math.sqrt(SAMPLES))
    high, low = split(rv[...])
    rhs[0:64] = high
    rhs[64:128] = high
    rhs[128:192] = low
    rhs[192:256] = jnp.zeros((64, 2 * TR), BF16)

    await_bytes(lab1, l1r)
    pltpu.make_async_copy(lab1, lab2.at[y], l2r).start()

    def tell_y(dy, c):
        remote(lab1, lab2.at[y], l2s, l2r, at(z, lax.rem(y + dy, NY), o)).start()
        return c

    lax.fori_loop(1, NY, tell_y, 0)

    weight = fold[...].astype(F32)
    part = NY // 2 * ROWS

    def transform(do, c):
        oo = lax.rem(o + do, NO)
        pltpu.make_async_copy(tab.at[oo], tv.at[do], tsem.at[do]).wait()
        pltpu.make_async_copy(gtab.at[oo], gv.at[do], gsem.at[do]).wait()
        short = dot(gv[do], rhs[...], 1, 0)
        for parity in range(2):
            four = dot(tv[do, parity], x2[parity], 1, 1)
            spec = (four[:part, :TR] + four[part:, TR:]) + (four[:part, TR:] + four[part:, :TR])
            for i in range(NY // 2):
                s = parity * (NY // 2) + i
                xr, xi = spec[i * ROWS : i * ROWS + 8], spec[i * ROWS + 8 : i * ROWS + 16]
                own = short[s * ROWS : (s + 1) * ROWS]
                gr, gi = 1.0 - own[:8, :TR], -own[8:, :TR]
                sbuf[do * NY + s, 0:8] = (xr * gr - xi * gi + own[:8, TR:]) * weight
                sbuf[do * NY + s, 8:16] = (xr * gi + xi * gr + own[8:, TR:]) * weight

        def send(dy, c):
            yy = lax.rem(y + dy, NY)
            src, dst = sbuf.at[do * NY + yy], rbuf.at[do * NY + dy]
            own = (do == 0) & (dy == 0)

            @pl.when(own)
            def _():
                pltpu.make_async_copy(src, dst, arecv.at[do]).start()

            @pl.when(jnp.logical_not(own))
            def _():
                remote(src, dst, asend, arecv.at[do], at(z, yy, oo)).start()

            return c

        lax.fori_loop(0, NY, send, 0)
        return c

    lax.fori_loop(0, NO, transform, 0)

    rest, coeff = pred[...], jnp.zeros((NY * ROWS, LAGS), F32)
    for _ in range(3):
        high = rest.astype(BF16)
        rest = rest - high.astype(F32)
        coeff = coeff + dot(place[...], high, 1, 1)
    cv[...] = coeff
    own = cv[pl.ds(pl.multiple_of(y * ROWS, ROWS), ROWS), :]
    for lag in range(LAGS):
        cb[lag] = jnp.broadcast_to(own[:, lag : lag + 1], (ROWS, 128))

    await_bytes(lab2, l2r)
    acc[...] = jnp.zeros_like(acc)
    which = lax.broadcasted_iota(jnp.int32, (GB, TR), 0)
    which8 = lax.broadcasted_iota(jnp.int32, (16, TR), 0)

    def stack(g, c):
        await_bytes(rbuf.at[pl.ds(g * NY, NY)], arecv.at[g])
        oo = lax.rem(o - g + NO, NO)
        for dy in range(NY):
            yy = lax.rem(y - dy + NY, NY)
            names = lab2[yy, oo, 0:1, :]
            folds = lab2[yy, oo, 1:2, :].astype(F32)
            upper, lower = lax.shift_right_logical(names, int(math.log2(GB))), names & (GB - 1)
            high, low = split(rbuf[g * NY + dy])
            high, low = high.astype(F32), low.astype(F32)
            lanes = slice(dy * TR, (dy + 1) * TR)
            for zz in range(NZ):
                here = upper == zz
                lhs[zz * ROWS : (zz + 1) * ROWS, lanes] = jnp.where(here, high, 0.0).astype(BF16)
                lhs[(NZ + zz) * ROWS : (NZ + zz + 1) * ROWS, lanes] = jnp.where(
                    here, low, 0.0
                ).astype(BF16)
            lhs[2 * NZ * ROWS :, lanes] = jnp.where(which8 == upper, folds, 0.0).astype(BF16)
            hot[:, lanes] = jnp.where(which == lower, 1.0, 0.0).astype(BF16)
        acc[...] += dot(lhs[...], hot[...], 1, 1)
        return c

    lax.fori_loop(0, NO, stack, 0)

    obuf[0, :, 0:128] = jnp.zeros((ROWS, 128), F32)
    fbuf[0, :, 0:128] = jnp.zeros((1, 128), F32)
    for zz in range(NZ):
        total = acc[zz * ROWS : (zz + 1) * ROWS] + acc[(NZ + zz) * ROWS : (NZ + zz + 1) * ROWS]
        folds = acc[2 * NZ * ROWS + zz : 2 * NZ * ROWS + zz + 1]
        obuf[zz, :, 128:] = total
        fbuf[zz, :, 128:] = folds
        if zz + 1 < NZ:
            obuf[zz + 1, :, 0:128] = total[:, GB - 128 :]
            fbuf[zz + 1, :, 0:128] = folds[:, GB - 128 :]

    def send_z(dz, c):
        zz = lax.rem(z + dz, NZ)
        remote(obuf.at[zz], obox.at[dz], bsend, brecv, at(zz, y, o)).start()
        remote(fbuf.at[zz], fbox.at[dz], fsend, frecv, at(zz, y, o)).start()
        return c

    lax.fori_loop(1, NZ, send_z, 0)
    total, folds = obuf[z], fbuf[z]
    await_bytes(fbox.at[pl.ds(1, NZ - 1)], frecv)
    for dz in range(1, NZ):
        folds = folds + fbox[dz]
    scale = 1.0 / jnp.sqrt(1.0 + folds)
    await_bytes(obox.at[pl.ds(1, NZ - 1)], brecv)
    for dz in range(1, NZ):
        total = total + obox[dz]
    normal = total * scale
    re, im = normal[:8], normal[8:]
    err_re, err_im = re[:, 128:], im[:, 128:]
    for lag in range(1, LAGS + 1):
        lag_re = pltpu.roll(re, lag, 1)[:, 128:]
        lag_im = pltpu.roll(im, lag, 1)[:, 128:]
        ar = jnp.concatenate([cb[lag - 1, 0:8]] * (GB // 128), axis=1)
        ai = jnp.concatenate([cb[lag - 1, 8:16]] * (GB // 128), axis=1)
        err_re = err_re - (ar * lag_re - ai * lag_im)
        err_im = err_im - (ar * lag_im + ai * lag_re)
    for tile in range(GB // 128):
        ebuf[tile, 0:8] = err_re[:, tile * 128 : (tile + 1) * 128]
        ebuf[tile, 8:16] = err_im[:, tile * 128 : (tile + 1) * 128]

    per_tile = 128 // BIN_DEV
    pltpu.make_async_copy(ebuf.at[lax.div(y, per_tile)], ebox.at[y], erecv).start()

    def send_y(dy, c):
        yy = lax.rem(y + dy, NY)
        remote(ebuf.at[lax.div(yy, per_tile)], ebox.at[y], esend, erecv, at(z, yy, o)).start()
        return c

    lax.fori_loop(1, NY, send_y, 0)
    await_bytes(ebox, erecv)
    rest = ebox[...].reshape(NY * ROWS, 128).T
    done = jnp.zeros((128, NY * ROWS), F32)
    for _ in range(3):
        high = rest.astype(BF16)
        rest = rest - high.astype(F32)
        done = done + dot(high, place[...], 1, 0)
    res[...] = done
    out[...] = res[pl.ds(pl.multiple_of(lax.rem(y, per_tile) * BIN_DEV, BIN_DEV), BIN_DEV), :]

    await_bytes(lab1.at[pl.ds(0, NO - 1)], l1s)
    await_bytes(lab2.at[pl.ds(0, NY - 1)], l2s)
    await_bytes(sbuf.at[pl.ds(0, NO * NY - 1)], asend)
    await_bytes(obuf.at[pl.ds(0, NZ - 1)], bsend)
    await_bytes(fbuf.at[pl.ds(0, NZ - 1)], fsend)
    await_bytes(ebox.at[pl.ds(0, NY - 1)], esend)


def on_device(traces, trace_dest, trace_bin, trace_class, trace_fold, filters, predictor):
    main, short, place = tables()
    vmem, far = pl.BlockSpec(memory_space=pltpu.VMEM), pl.BlockSpec(memory_space=pl.ANY)
    dma, box = pltpu.SemaphoreType.DMA, pltpu.VMEM
    return pl.pallas_call(
        kernel,
        out_shape=jax.ShapeDtypeStruct((BIN_DEV, NY * ROWS), F32),
        in_specs=[far] + [vmem] * 6 + [far, far, vmem],
        out_specs=vmem,
        scratch_shapes=[
            box((TR, SAMPLES), F32),
            box(main.shape, BF16),
            box(short.shape, BF16),
            box((2, 2 * TR, HALF), BF16),
            box((2 * TAPS, TR), F32),
            box((64, 2 * TR), F32),
            box((256, 2 * TR), BF16),
            box((2, TR), jnp.int32),
            box((NO, 2, TR), jnp.int32),
            box((NY, NO, 2, TR), jnp.int32),
            box((NO * NY, ROWS, TR), F32),
            box((NO * NY, ROWS, TR), F32),
            box((2 * NZ * ROWS + 16, NY * TR), BF16),
            box((GB, NY * TR), BF16),
            box((2 * NZ * ROWS + 16, GB), F32),
            box((NZ, ROWS, WIDE), F32),
            box((NZ, ROWS, WIDE), F32),
            box((NZ, 1, WIDE), F32),
            box((NZ, 1, WIDE), F32),
            box((GB // 128, ROWS, 128), F32),
            box((NY, ROWS, 128), F32),
            box((NY * ROWS, LAGS), F32),
            box((LAGS, ROWS, 128), F32),
            box((128, NY * ROWS), F32),
            dma,
            dma((NO,)),
            dma((NO,)),
            dma, dma, dma, dma, dma,
            dma((NO,)),
            dma, dma, dma, dma, dma, dma,
        ],
        compiler_params=pltpu.CompilerParams(
            collective_id=0, has_side_effects=True, vmem_limit_bytes=40 * 2**20
        ),
        cost_estimate=pl.CostEstimate(flops=2 * 10**9, bytes_accessed=5 * 10**6, transcendentals=0),
    )(
        traces, trace_dest.reshape(1, TR), trace_bin, trace_class, trace_fold, filters, predictor,
        jnp.asarray(main), jnp.asarray(short), jnp.asarray(place),
    )


def solution(mesh):
    in_specs = (
        P("off", "bin", None),
        P("off", "bin", None),
        P("off", "bin"),
        P("off", "bin"),
        P("off", "bin"),
        P(),
        P(None, "off"),
    )
    return jax.shard_map(
        on_device, mesh=mesh, in_specs=in_specs, out_specs=P("bin", "off"), check_vma=False
    )
```

time: 264 us -> 62 us (0.23); the launches traced: 259 us -> 61.5 us
  waiting for transfers between devices: 138 us -> 0 us
  Pallas kernels: 0 us -> 52.1 us
  other arithmetic: 38.5 us -> 0 us
  starting transfers between devices: 25.4 us -> 0 us
  local copies, waits for them, and re-layouts: 24.3 us -> 9.43 us
  blocking collectives: 14.5 us -> 0 us
  between operations: 13.9 us -> 0.02 us
  matrix products: 4.26 us -> 0 us
    psum x1 -> x0, waiting for transfers between devices: 81.6 us -> none  [on_device(): stacked, fold_total = lax.psum((stacked, fold_total), 'off')]
    all_to_all x2 -> x0, waiting for transfers between devices: 56.2 us -> none  [the longest x1 48.3 us: on_device(): lax.all_to_all(outbox.reshape(bin_devices, capacity, samples), 'bin', spl...]
    pallas_call x0 -> x1, Pallas kernels: none -> 52.1 us  [on_device(): pl.pallas_call(kernel, out_shape=jax.ShapeDtypeStruct((BIN_DEV, NY * ROWS...]
    dot_general x1 -> x0, other arithmetic: 33.2 us -> none  [stack_rows(): jnp.dot(placing, flattened, precision=lax.Precision.HIGHEST, preferred_el...]
    all_to_all x2 -> x0, starting transfers between devices: 22.7 us -> none  [the longest x1 17.1 us: on_device(): lax.all_to_all(label_box, 'bin', split_axis=0, concat_axis=0, tiled=True)]
    psum x1 -> x0, blocking collectives: 14.5 us -> none  [on_device(): stacked, fold_total = lax.psum((stacked, fold_total), 'off')]
    slice x39 -> x0, local copies, waits for them, and re-layouts: 10.7 us -> none  [the longest x1 4.7 us: on_device(): coeff_real = coeffs[lag_index - 1, :, 0]]
    reshape x7 -> x0, local copies, waits for them, and re-layouts: 7.59 us -> none  [the longest x1 2.62 us: on_device(): flattened = part_records.reshape(-1, samples)]
  transfers between devices with their start and end apart: 4 -> 0, of which waited for: 4 -> 0; matrix products, arithmetic and copies ran while one was open for 6% -> 0% of each run, Pallas kernels for 0% -> 0%
where the time goes in v1:
time: 62 us; the launch traced here: 61.5 us
  Pallas kernels  52.1 us (84%)
  local copies, waits for them, and re-layouts  9.43 us (15%)
    pallas_call x1, Pallas kernels, on_device(): pl.pallas_call(kernel, out_shape=jax.ShapeDtypeStruct((BIN_DEV, NY * ROWS...  52.1 us
    unnamed x21, local copies, waits for them, and re-layouts  9.43 us

profile of v1, /device:TPU:1, one launch (start us, length us, event | category | flops | bytes accessed | tf_op | source)
XLA Modules:
  0.0 61.5 jit_solution(18130534284627056049)
XLA Ops:
  0.0 0.0 copy-start
  0.0 1.1 %copy-done = f32[1,128,1536]{2,1,0:T(8,128)S(1)} copy-done((f32[1,128,1536]{2,1,0:T(8,128)S(1)}, f32[1,128,1536]{2,1,0:T(8,128)}, u32[]{:S(2)}) %copy-start) | copy-done | bytes 786456
  1.1 0.0 copy-start.1
  1.1 0.7 %copy-done.1 = f32[16,128]{1,0:T(8,128)S(1)} copy-done((f32[16,128]{1,0:T(8,128)S(1)}, f32[16,128]{1,0:T(8,128)}, u32[]{:S(2)}) %copy-start.1) | copy-done | bytes 8216
  1.8 0.0 copy-start.2
  1.8 0.7 %copy-done.2 = f32[8,48]{1,0:T(8,128)S(1)} copy-done((f32[8,48]{1,0:T(8,128)S(1)}, f32[8,48]{1,0:T(8,128)}, u32[]{:S(2)}) %copy-start.2) | copy-done | bytes 1560
  2.5 0.0 copy-start.3
  2.5 0.7 %copy-done.3 = s32[1,128,1]{1,2,0:T(1,128)S(1)} copy-done((s32[1,128,1]{1,2,0:T(1,128)S(1)}, s32[1,128,1]{1,2,0:T(1,128)}, u32[]{:S(2)}) %copy-start.3) | copy-done | bytes 536
  3.2 0.0 copy-start.4
  3.2 0.7 %copy-done.4 = s32[1,128]{1,0:T(1,128)S(1)} copy-done((s32[1,128]{1,0:T(1,128)S(1)}, s32[1,128]{1,0:T(1,128)}, u32[]{:S(2)}) %copy-start.4) | copy-done | bytes 536
  3.8 0.0 copy-start.5
  3.8 0.7 %copy-done.5 = s32[1,128]{1,0:T(1,128)S(1)} copy-done((s32[1,128]{1,0:T(1,128)S(1)}, s32[1,128]{1,0:T(1,128)}, u32[]{:S(2)}) %copy-start.5) | copy-done | bytes 536
  4.5 0.0 copy-start.6
  4.5 0.7 %copy-done.6 = s32[1,128]{1,0:T(1,128)S(1)} copy-done((s32[1,128]{1,0:T(1,128)S(1)}, s32[1,128]{1,0:T(1,128)}, u32[]{:S(2)}) %copy-start.6) | copy-done | bytes 536
  5.1 0.0 copy-start.7
  5.1 1.9 %copy-done.7 = bf16[8,2,128,768]{3,2,1,0:T(8,128)(2,1)S(1)} copy-done((bf16[8,2,128,768]{3,2,1,0:T(8,128)(2,1)S(1)}, bf16[8,2,128,768]{3,2,1,0:T(8,128)(2,1)}, u32[]{:S(2)}) %copy-start.7) | copy-done | bytes 3145752
  7.0 0.0 copy-start.8
  7.0 1.0 %copy-done.8 = bf16[8,128,256]{2,1,0:T(8,128)(2,1)S(1)} copy-done((bf16[8,128,256]{2,1,0:T(8,128)(2,1)S(1)}, bf16[8,128,256]{2,1,0:T(8,128)(2,1)}, u32[]{:S(2)}) %copy-start.8) | copy-done | bytes 524312
  8.1 0.0 copy-start.9
  8.1 0.8 %copy-done.9 = bf16[128,128]{1,0:T(8,128)(2,1)S(1)} copy-done((bf16[128,128]{1,0:T(8,128)(2,1)S(1)}, bf16[128,128]{1,0:T(8,128)(2,1)}, u32[]{:S(2)}) %copy-start.9) | copy-done | bytes 32792
  8.8 52.1 %shard_map.100 = f32[32,128]{1,0:T(8,128)S(1)} custom-call(f32[1,128,1536]{2,1,0:T(8,128)S(1)} %copy-done, s32[1,128]{1,0:T(1,128)S(1)} %bitcast.1, s32[1,128]{1,0:T(1,128)S(1)} %copy-done.4, s32[1,128]{1,0:T(1,128)S(1)} %copy-done.5, s32[1,128]{1,0:T(1,128)S(1)} %copy-done.6, f32[8,48]{1,0:T(8,128)S(1)} %copy-done.2, f32[16,128]{1,0:T(8,128)S(1)} %copy-done.1, ...), custom_call_target="tpu_custom_call" | custom-call | flops 2000000000 | bytes 5000000 | tf_op jit(solution)/shard_map/pallas_call | solution.py:305
  60.9 0.6 copy.12
Async XLA Ops:
  0.0 1.1 %copy-start = (f32[1,128,1536]{2,1,0:T(8,128)S(1)}, f32[1,128,1536]{2,1,0:T(8,128)}, u32[]{:S(2)}) copy-start(f32[1,128,1536]{2,1,0:T(8,128)} %traces.1) | copy-start | bytes 2359300
  1.1 0.7 %copy-start.1 = (f32[16,128]{1,0:T(8,128)S(1)}, f32[16,128]{1,0:T(8,128)}, u32[]{:S(2)}) copy-start(f32[16,128]{1,0:T(8,128)} %pred_.1) | copy-start | bytes 24580
  1.8 0.7 %copy-start.2 = (f32[8,48]{1,0:T(8,128)S(1)}, f32[8,48]{1,0:T(8,128)}, u32[]{:S(2)}) copy-start(f32[8,48]{1,0:T(8,128)} %filt.1) | copy-start | bytes 4612
  2.5 0.7 %copy-start.3 = (s32[1,128,1]{1,2,0:T(1,128)S(1)}, s32[1,128,1]{1,2,0:T(1,128)}, u32[]{:S(2)}) copy-start(s32[1,128,1]{1,2,0:T(1,128)} %param.11) | copy-start | bytes 1540
  3.2 0.7 %copy-start.4 = (s32[1,128]{1,0:T(1,128)S(1)}, s32[1,128]{1,0:T(1,128)}, u32[]{:S(2)}) copy-start(s32[1,128]{1,0:T(1,128)} %slot.1) | copy-start | bytes 1540
  3.8 0.7 %copy-start.5 = (s32[1,128]{1,0:T(1,128)S(1)}, s32[1,128]{1,0:T(1,128)}, u32[]{:S(2)}) copy-start(s32[1,128]{1,0:T(1,128)} %cls.1) | copy-start | bytes 1540
  4.5 0.7 %copy-start.6 = (s32[1,128]{1,0:T(1,128)S(1)}, s32[1,128]{1,0:T(1,128)}, u32[]{:S(2)}) copy-start(s32[1,128]{1,0:T(1,128)} %fold.1) | copy-start | bytes 1540
  5.1 1.9 %copy-start.7 = (bf16[8,2,128,768]{3,2,1,0:T(8,128)(2,1)S(1)}, bf16[8,2,128,768]{3,2,1,0:T(8,128)(2,1)}, u32[]{:S(2)}) copy-start(bf16[8,2,128,768]{3,2,1,0:T(8,128)(2,1)} %constant.6.clone.tab) | copy-start | bytes 9437188
  7.0 1.0 %copy-start.8 = (bf16[8,128,256]{2,1,0:T(8,128)(2,1)S(1)}, bf16[8,128,256]{2,1,0:T(8,128)(2,1)}, u32[]{:S(2)}) copy-start(bf16[8,128,256]{2,1,0:T(8,128)(2,1)} %constant.7.clone.gtab) | copy-start | bytes 1572868
  8.1 0.8 %copy-start.9 = (bf16[128,128]{1,0:T(8,128)(2,1)S(1)}, bf16[128,128]{1,0:T(8,128)(2,1)}, u32[]{:S(2)}) copy-start(bf16[128,128]{1,0:T(8,128)(2,1)} %constant.8.clone.place) | copy-start | bytes 98308
